TPU v7x, 256 devices: a whole 4x4x8 slice. The times are simulated.
256 devices in a mesh: ind: 8 (over x, core), var: 32 (over y, z).
Axes of the slice: x: 4, y: 4, z: 8, core: 2. Of those that a mesh axis runs over, the one named last changes fastest.
Arguments:
- genotypes: bfloat16 [12288, 102400], P('ind', 'var'), may hold values from -0.0546875 to 0.0546875
- phenotype: float32 [12288, 192], P('ind'), may hold values from -40 to 40, as said below
- beta_start: float32 [192, 102400], P('ind', 'var'), may hold values from -5 to 5, as said below
- penalty: float32 [192], replicated, may hold values from 0.5 to 4
- step_size: float32 [1], replicated, may hold values from 0.02 to 0.06
Outputs:
- beta_final: float32 [192, 102400], P('ind', 'var')
- objective: float32 [2, 192], replicated
Inputs may be any that keep to these rules, and one draw needn't show every extreme that they name: `phenotype`: Real-valued phenotypes. `beta_start`: Real-valued warm-start coefficients, a part of them exactly zero.
All inputs are finite; a program needn't handle non-finite values.
Results may differ from a plain program's by a relative error of at most 0.00087.
Values may be sent and summed in bfloat16 or wider, within the bound.
A program may use at most 64 MiB of HBM per device.

v0:
```python
import jax
import jax.numpy as jnp
from jax import lax
from jax.sharding import PartitionSpec as P

ITERS = 2


def on_device(genotypes, phenotype, beta_start, penalty, step_size):
    tile_rows = genotypes.shape[0]
    traits_local = beta_start.shape[0]
    traits_all = traits_local * lax.axis_size("ind")
    total_rows = jnp.float32(tile_rows * lax.axis_size("ind"))
    trait_offset = lax.axis_index("ind") * traits_local
    penalty_local = lax.dynamic_slice_in_dim(penalty, trait_offset, traits_local, 0)
    scale = step_size[0]
    beta = beta_start
    records = []
    for iteration in range(ITERS):
        coef_half = beta.astype(jnp.bfloat16)
        partial_pred = lax.dot_general(
            genotypes,
            lax.all_gather(coef_half, "ind", axis=0, tiled=True),
            (((1,), (1,)), ((), ())),
            preferred_element_type=jnp.float32,
        )
        predictor = lax.psum(partial_pred, "var")
        residual = phenotype - predictor
        leader = (lax.axis_index("var") == 0).astype(jnp.float32)
        loss_term = 0.5 * jnp.sum(residual * residual, axis=0) * leader
        residual_half = residual.astype(jnp.bfloat16)
        penalty_sum = penalty_local * jnp.sum(jnp.abs(beta), axis=1)
        penalty_term = lax.dynamic_update_slice_in_dim(
            jnp.zeros((traits_all,), jnp.float32), penalty_sum, trait_offset, 0
        )
        step_term = (loss_term + penalty_term) / total_rows
        records.append(lax.psum(step_term, ("ind", "var")))
        partial_grad = lax.dot_general(
            residual_half, genotypes, (((0,), (0,)), ((), ())), preferred_element_type=jnp.float32
        )
        summed_grad = lax.psum(partial_grad, "ind")
        ascent = lax.dynamic_slice_in_dim(summed_grad, trait_offset, traits_local, 0)
        moved = beta + scale * ascent
        beta = jnp.sign(moved) * jnp.maximum(jnp.abs(moved) - scale * penalty_local[:, None], 0.0)
    objective = jnp.stack(records, axis=0)
    return (beta, objective)


def solution(mesh):
    placed = (P("ind", "var"), P("ind", None), P("ind", "var"), P(), P())
    return jax.shard_map(
        on_device, mesh=mesh, in_specs=placed, out_specs=(P("ind", "var"), P()), check_vma=False
    )
```

profile of v0, /device:TPU:1, one launch (start us, length us, event | category | flops | bytes accessed | tf_op | source)
XLA Modules:
  0.0 557.4 jit_solution(3185798254959484746)
XLA Ops:
  7.2 0.0 all-gather.3.cloned.1.call-start
  7.2 1.9 abs_reduce_fusion.1
  9.1 0.0 all-gather.3.cloned.1.call-update
  9.1 0.0 all-reduce.6.cloned.1.call-start
  9.2 31.7 %all-gather.3.cloned.1.call-done = bf16[192,3200]{1,0:T(8,128)(2,1)} async-done(((bf16[24,3200]{1,0:T(8,128)(2,1)}), bf16[192,3200]{1,0:T(8,128)(2,1)}) %all-gather.3.cloned.1.call-update) | async-done | bytes 1228816 | tf_op jit(solution)/shard_map/all_gather | solution.py:23
  40.9 8.6 %fusion.6 = f32[1536,192]{0,1:T(8,128)} fusion(bf16[1536,3200]{1,0:T(8,128)(2,1)} %param.5, bf16[192,3200]{1,0:T(8,128)(2,1)} %all-gather.3.cloned.1.call-done), kind=kOutput, calls=%fused_computation.21 | convolution fusion | flops 1887436800 | bytes 12238848 | tf_op jit(solution)/shard_map/dot_general | solution.py:21
  49.5 0.0 all-reduce.6.cloned.1.call-update
  49.5 0.0 all-reduce.8.cloned.1.call-start
  49.6 144.9 %all-reduce.6.cloned.1.call-done = f32[1536,192]{0,1:T(8,128)} async-done(((f32[1536,192]{0,1:T(8,128)}), f32[1536,192]{0,1:T(8,128)}) %all-reduce.6.cloned.1.call-update) | async-done | bytes 1179664 | tf_op jit(solution)/shard_map/psum | solution.py:27
  194.5 7.8 %fusion.2 = f32[192,3200]{1,0:T(8,128)} fusion(bf16[1536,3200]{1,0:T(8,128)(2,1)} %param.5, f32[1536,192]{0,1:T(8,128)S(1)} %copy-done, f32[1536,192]{0,1:T(8,128)} %all-reduce.6.cloned.1.call-done), kind=kOutput, calls=%fused_computation.5 | convolution fusion | flops 1888026624 | bytes 14647296 | tf_op jit(solution)/shard_map/dot_general | solution.py:38
  202.3 0.0 all-reduce.8.cloned.1.call-update
  202.3 0.0 all-gather.5.cloned.1.call-start
  203.1 0.1 broadcast_multiply_fusion.4
  203.1 71.2 %all-reduce.8.cloned.1.call-done = f32[192,3200]{1,0:T(8,128)} async-done(((f32[192,3200]{1,0:T(8,128)}), f32[192,3200]{1,0:T(8,128)}) %all-reduce.8.cloned.1.call-update) | async-done | bytes 2457616 | tf_op jit(solution)/shard_map/psum | solution.py:41
  274.3 1.2 abs_reduce_fusion
  275.6 0.7 copy-done.3
  276.3 0.7 convert_element_type.16
  277.0 0.0 all-gather.5.cloned.1.call-update
  277.0 0.0 all-reduce.10.cloned.1.call-start
  277.0 28.4 %all-gather.5.cloned.1.call-done = bf16[192,3200]{1,0:T(8,128)(2,1)} async-done(((bf16[24,3200]{1,0:T(8,128)(2,1)}), bf16[192,3200]{1,0:T(8,128)(2,1)}) %all-gather.5.cloned.1.call-update) | async-done | bytes 1228816 | tf_op jit(solution)/shard_map/all_gather | solution.py:23
  305.4 8.6 %convolution_bitcast_fusion = f32[1536,192]{0,1:T(8,128)} fusion(bf16[192,3200]{1,0:T(8,128)(2,1)} %all-gather.5.cloned.1.call-done, bf16[1536,3200]{1,0:T(8,128)(2,1)} %param.5), kind=kOutput, calls=%fused_computation | convolution fusion | flops 1887436800 | bytes 12238848 | tf_op jit(solution)/shard_map/dot_general | solution.py:21
  314.0 0.0 all-reduce.12.cloned.1.call-start
  314.1 144.8 %all-reduce.10.cloned.1.call-done = f32[1536,192]{0,1:T(8,128)} async-done(((f32[1536,192]{0,1:T(8,128)}), f32[1536,192]{0,1:T(8,128)}) %all-reduce.10.cloned.1.call-update) | async-done | bytes 1179664 | tf_op jit(solution)/shard_map/psum | solution.py:27
  458.9 7.8 %fusion = f32[192,3200]{1,0:T(8,128)} fusion(bf16[1536,3200]{1,0:T(8,128)(2,1)} %param.5, f32[1536,192]{0,1:T(8,128)S(1)} %copy-done, f32[1536,192]{0,1:T(8,128)} %all-reduce.10.cloned.1.call-done), kind=kOutput, calls=%fused_computation.3 | convolution fusion | flops 1888026624 | bytes 14647296 | tf_op jit(solution)/shard_map/dot_general | solution.py:38
  466.7 0.0 all-reduce.12.cloned.1.call-update
  466.7 1.2 copy-done.1
  468.0 0.4 copy-done.2
  468.3 0.4 multiply_reduce_fusion.1
  468.7 0.2 add_dynamic-update-slice_fusion.1
  468.9 79.1 %all-reduce = (f32[1,192]{1,0:T(1,128)S(1)}, f32[1,192]{1,0:T(1,128)S(1)}) all-reduce(f32[1,192]{1,0:T(1,128)S(1)} %bitcast.15, f32[1,192]{1,0:T(1,128)S(1)} %bitcast.14), channel_id=1, replica_groups=mesh['ind'=8,'var'=32] {'ind','var'}, use_global_device_ids=true, to_apply=%region_9.0 | all-reduce | flops 384 | bytes 3072 | tf_op jit(solution)/shard_map/psum | solution.py:37
  548.0 0.6 pad_maximum_fusion
  548.6 1.9 maximum_multiply_fusion
  (14 shorter events, 0.0 us)
Async XLA Ops:
  7.2 33.8 %all-gather.3.cloned.1.call-start = ((), (), s32[]{:S(2)}) async-start(), calls=%async_computation | async-start | bytes 1382400 | tf_op jit(solution)/shard_map/all_gather | solution.py:23
  9.1 185.4 %all-reduce.6.cloned.1.call-start = ((), (), s32[]{:S(2)}) async-start(), calls=%async_computation.1 | async-start | bytes 2359296 | tf_op jit(solution)/shard_map/psum | solution.py:27
  49.5 145.0 %copy-start = (f32[1536,192]{0,1:T(8,128)S(1)}, f32[1536,192]{0,1:T(8,128)}, u32[]{:S(2)}) copy-start(f32[1536,192]{0,1:T(8,128)} %param.6) | copy-start | bytes 3538948
  49.5 224.8 %all-reduce.8.cloned.1.call-start = ((), (), s32[]{:S(2)}) async-start(), calls=%async_computation.2 | async-start | bytes 4915200 | tf_op jit(solution)/shard_map/psum | solution.py:41
  202.3 0.8 copy-start.5
  202.3 72.0 %copy-start.4 = (f32[24,3200]{1,0:T(8,128)S(1)}, f32[24,3200]{1,0:T(8,128)}, u32[]{:S(2)}) copy-start(f32[24,3200]{1,0:T(8,128)} %param.7) | copy-start | bytes 921604
  202.3 103.1 %all-gather.5.cloned.1.call-start = ((), (), s32[]{:S(2)}) async-start(), calls=%async_computation.3 | async-start | bytes 1382400 | tf_op jit(solution)/shard_map/all_gather | solution.py:23
  275.6 0.7 copy-start.3
  277.0 181.9 %all-reduce.10.cloned.1.call-start = ((), (), s32[]{:S(2)}) async-start(), calls=%async_computation.4 | async-start | bytes 2359296 | tf_op jit(solution)/shard_map/psum | solution.py:27
  314.0 234.6 %all-reduce.12.cloned.1.call-start = ((), (), s32[]{:S(2)}) async-start(), calls=%async_computation.5 | async-start | bytes 4915200 | tf_op jit(solution)/shard_map/psum | solution.py:41
  466.7 1.3 copy-start.1
  466.7 1.6 copy-start.2
Sparse Core Ops, SparseCore 0:
  10.4 30.4 all-gather.2
  49.7 144.7 all-reduce.5
  202.4 71.8 all-reduce.7
  277.1 28.2 all-gather.4
  314.1 144.7 all-reduce.9
  466.8 72.2 all-reduce.11
where the time goes:
time: 558 us; the launch traced here: 557 us
  waiting for transfers between devices  421 us (75%)
  blocking collectives  79.1 us (14%)
  matrix products  32.8 us (6%)
  between operations  14.8 us (3%)
  other arithmetic  6.96 us (1%)
    psum x2, waiting for transfers between devices, on_device(): predictor = lax.psum(partial_pred, 'var')  290 us
    psum x1, blocking collectives, on_device(): records.append(lax.psum(step_term, ('ind', 'var')))  79.1 us
    psum x2, waiting for transfers between devices, on_device(): summed_grad = lax.psum(partial_grad, 'ind')  71.2 us
    all_gather x2, waiting for transfers between devices, on_device(): lax.all_gather(coef_half, 'ind', axis=0, tiled=True)  60.1 us
    dot_general x2, matrix products, on_device(): lax.dot_general(genotypes, lax.all_gather(coef_half, 'ind', axis=0, tiled...  17.2 us
    dot_general x2, matrix products, on_device(): lax.dot_general(residual_half, genotypes, (((0,), (0,)), ((), ())), prefe...  15.6 us
  transfers between devices with their start and end apart: 6, of which 5 were waited for; matrix products, arithmetic and copies ran while one was open for 0% of the time, Pallas kernels for 0%

commit v1 on v0

v1 whole, which is shorter than its diff:
```python
import functools

import jax
import jax.numpy as jnp
from jax import lax
from jax.experimental import pallas as pl
from jax.experimental.pallas import tpu as pltpu
from jax.sharding import PartitionSpec as P

ITERS = 2
X, C, Y, Z = 4, 2, 4, 8
GROUPS = 3
R8 = 8
ROWS, COLS = 1536, 3200
TRAITS = 192
LOCAL = TRAITS // (X * C)
GT = R8 * X * C
CHUNK = ROWS // Y
LO = 1664
HI = COLS - LO
MESH = pl.DeviceIdType.MESH
F32, BF16 = jnp.float32, jnp.bfloat16
NT = (((1,), (1,)), ((), ()))
NN = (((1,), (0,)), ((), ()))
COL_CHUNK = 640


def kernel(
    step_ref, pen_ref, geno, pheno, beta0, out_beta, out_obj,
    g_buf, ph_in, ph_t, beta, stat, stat_y, stat_z, stat_x, stat_c,
    cb, coef, pp, ry, sz, rz, az, rt, gp, pr, ps, rx,
    load_sem,
    agx_s, agx_r, rel_s, rel_r, rsy_s, rsy_r, rsz_s, rsz_r, agz_s, agz_r, agy_s, agy_r, pair_s, pair_r, rsx_s, rsx_r,
    ob_s, ob_r,
):
    ind, var = lax.axis_index("ind"), lax.axis_index("var")
    x, c = ind // C, ind % C
    y, z = var // Z, var % Z

    def at_x(k):
        return (((x + k) % X) * C + c, var)

    def at_y(k):
        return (ind, ((y + k) % Y) * Z + z)

    def at_z(k):
        return (ind, y * Z + (z + k) % Z)

    peer = (x * C + (1 - c), var)

    loads = []
    beta_load = pltpu.make_async_copy(beta0, beta, load_sem.at[0])
    beta_load.start()
    for n, k in enumerate((2, 1, 3, 0)):
        rows = pl.ds(pl.multiple_of(((y + k) % Y) * CHUNK, CHUNK), CHUNK)
        load = pltpu.make_async_copy(geno.at[rows, :], g_buf.at[pl.ds(k * CHUNK, CHUNK), :], load_sem.at[2 + n])
        loads.append(load)
    loads[0].start()
    rows = pl.ds(pl.multiple_of(y * CHUNK, CHUNK), CHUNK)
    ph_load = pltpu.make_async_copy(pheno.at[rows, :], ph_in, load_sem.at[1])
    ph_load.start()
    for load in loads[1:]:
        load.start()

    barrier = pltpu.get_barrier_semaphore()
    partners = [peer]
    partners += [at_x(k) for k in range(1, X)] + [at_y(k) for k in range(1, Y)] + [at_z(k) for k in range(1, Z)]
    for partner in partners:
        pl.semaphore_signal(barrier, inc=1, device_id=partner, device_id_type=MESH)
    pl.semaphore_wait(barrier, len(partners))

    scale = step_ref[0]
    lane = lax.broadcasted_iota(jnp.int32, (LOCAL, TRAITS), 1)
    row = lax.broadcasted_iota(jnp.int32, (LOCAL, TRAITS), 0)
    mine = lane == row + ind * LOCAL
    pen_col = jnp.sum(jnp.where(mine, pen_ref[...], 0.0), axis=1, keepdims=True)
    stat[...] = jnp.zeros_like(stat)
    s_lane = lax.broadcasted_iota(jnp.int32, (R8, 256), 1)
    s_row = lax.broadcasted_iota(jnp.int32, (R8, 256), 0)

    def add_stat(it, first, column):
        hit = s_lane == s_row + first
        stat[it : it + 1, :] += jnp.sum(jnp.where(hit, column, 0.0), axis=0, keepdims=True) * (1.0 / (ROWS * X * C))

    pending = {}

    def send(key, src, dst, s_sem, r_sem, device):
        copy = pltpu.make_async_remote_copy(
            src_ref=src, dst_ref=dst, send_sem=s_sem, recv_sem=r_sem, device_id=device, device_id_type=MESH
        )
        copy.start()
        pending.setdefault(key, []).append(copy)

    def receive(key, one=None):
        copies = pending[key] if one is None else [pending[key][one]]
        for copy in copies:
            copy.wait_recv()

    def settle(key):
        for copy in pending.pop(key, []):
            copy.wait_send()

    def send_coef(g, it):
        settle(("agx", g))
        b = beta[R8 * g : R8 * g + R8, :]
        add_stat(it, ind * LOCAL + R8 * g, pen_col[R8 * g : R8 * g + R8] * jnp.sum(jnp.abs(b), axis=1, keepdims=True))
        high = jnp.concatenate([b[:, LO:], jnp.zeros((R8, LO - HI), F32)], axis=1)
        cb[g, 0, 0] = jnp.concatenate([b[:, :LO], high], axis=0).astype(BF16)
        own = cb.at[g, 0, 0]
        for n, k in enumerate((2, 1, 3)):
            send(("agx", g), own, cb.at[g, k, 0], agx_s.at[g, n], agx_r.at[g, n], at_x(k))
        send(("agx", g), own, cb.at[g, 0, 1], agx_s.at[g, 3], agx_r.at[g, 3], peer)

    def t0(g, it):
        if g == 0:
            beta_load.wait()
        send_coef(g, 0)

    def t1(g, it):
        for n, k in ((1, 1), (2, 3), (0, 2)):
            receive(("agx", g), n)
            send(("rel", g), cb.at[g, k, 0], cb.at[g, k, 1], rel_s.at[g, k - 1], rel_r.at[g, k - 1], peer)

    def t2(g, it):
        receive(("agx", g), 3)
        receive(("rel", g))
        settle(("rsy", g))
        for k in range(X):
            a, b = cb[g, k, 0].astype(F32), cb[g, k, 1].astype(F32)
            rows = slice(2 * R8 * k, 2 * R8 * k + 2 * R8)
            coef[rows, :LO] = jnp.concatenate([a[:R8], b[:R8]], axis=0).astype(BF16)
            coef[rows, LO:] = jnp.concatenate([a[R8:, :HI], b[R8:, :HI]], axis=0).astype(BF16)
        for n, k in enumerate((2, 1, 3, 0)):
            if it == 0 and g == 0:
                loads[n].wait()
            pp[g, k] = lax.dot_general(
                coef[...], g_buf[CHUNK * k : CHUNK * k + CHUNK, :], NT, preferred_element_type=F32
            )
            if k:
                send(("rsy", g), pp.at[g, k], ry.at[g, k - 1], rsy_s.at[g, k - 1], rsy_r.at[g, k - 1], at_y(k))

    def t3(g, it):
        receive(("rsy", g))
        settle(("rsz", g))
        total = pp[g, 0] + ry[g, 0] + ry[g, 1] + ry[g, 2]
        sz[g] = total.reshape(Z, R8, CHUNK)
        for k in (4, 3, 5, 2, 6, 1, 7):
            send(("rsz", g), sz.at[g, (z + k) % Z], rz.at[g, k - 1], rsz_s.at[g, k - 1], rsz_r.at[g, k - 1], at_z(k))

    def t4(g, it):
        if it == 0 and g == 0:
            ph_load.wait()
            ph_t[...] = ph_in[...].T.reshape(X * C * GROUPS, R8, CHUNK)
        receive(("rsz", g))
        settle(("agz", g))
        total = sz[g, z]
        for k in range(Z - 1):
            total += rz[g, k]
        k, f = z // C, z % C
        owner = ((x - k + X) % X) * C + (c + f) % C
        residual = ph_t[owner * GROUPS + g] - total
        az[g, z] = residual
        add_stat(it, owner * LOCAL + R8 * g, 0.5 * jnp.sum(residual * residual, axis=1, keepdims=True))
        for k in (4, 3, 5, 2, 6, 1, 7):
            send(("agz", g), az.at[g, z], az.at[g, z], agz_s.at[g, k - 1], agz_r.at[g, k - 1], at_z(k))

    def t5(g, it):
        receive(("agz", g))
        settle(("agy", g))
        rt[g, :, :CHUNK] = az[g].reshape(GT, CHUNK).astype(BF16)
        for k in (2, 1, 3):
            m = (Y - k) % Y
            send(
                ("agy", g), rt.at[g, :, pl.ds(0, CHUNK)], rt.at[g, :, pl.ds(m * CHUNK, CHUNK)],
                agy_s.at[g, k - 1], agy_r.at[g, k - 1], at_y(k),
            )

    def t6(g, it):
        receive(("agy", g))
        settle(("pair", g))
        for s in range(0, COLS, COL_CHUNK):
            part = lax.dot_general(rt[g], g_buf[:, s : s + COL_CHUNK], NN, preferred_element_type=F32)
            gp[g, :, :, :, s : s + COL_CHUNK] = part.reshape(X, C, R8, COL_CHUNK)
        send(("pair", g), gp.at[g, :, 1], pr.at[g], pair_s.at[g], pair_r.at[g], peer)

    def t7(g, it):
        receive(("pair", g))
        settle(("rel", g))
        settle(("rsx", g))
        for k in (2, 1, 3, 0):
            ps[g, k] = gp[g, k, 0] + pr[g, k]
            if k:
                send(("rsx", g), ps.at[g, k], rx.at[g, k - 1], rsx_s.at[g, k - 1], rsx_r.at[g, k - 1], at_x(X - k))

    def t8(g, it):
        receive(("rsx", g))
        ascent = ps[g, 0] + rx[g, 0] + rx[g, 1] + rx[g, 2]
        rows = slice(R8 * g, R8 * g + R8)
        moved = beta[rows, :] + scale * ascent
        bound = scale * pen_col[rows]
        updated = moved - jnp.clip(moved, -bound, bound)
        if it == ITERS - 1:
            out_beta[rows, :] = updated
        else:
            beta[rows, :] = updated
            send_coef(g, it + 1)

    def o1():
        stat_y[y] = stat[...]
        for k in range(1, Y):
            send("oy", stat_y.at[y], stat_y.at[y], ob_s.at[k - 1], ob_r.at[k - 1], at_y(k))

    def o2():
        receive("oy")
        stat_z[z] = stat_y[0] + stat_y[1] + stat_y[2] + stat_y[3]
        for k in range(1, Z):
            send("oz", stat_z.at[z], stat_z.at[z], ob_s.at[2 + k], ob_r.at[2 + k], at_z(k))

    def o3():
        receive("oz")
        total = stat_z[0]
        for k in range(1, Z):
            total += stat_z[k]
        stat_x[x] = total
        for k in range(1, X):
            send("ox", stat_x.at[x], stat_x.at[x], ob_s.at[9 + k], ob_r.at[9 + k], at_x(k))

    def o4():
        receive("ox")
        stat_c[c] = stat_x[0] + stat_x[1] + stat_x[2] + stat_x[3]
        send("oc", stat_c.at[c], stat_c.at[c], ob_s.at[13], ob_r.at[13], peer)

    def o5():
        receive("oc")
        total = stat_c[0] + stat_c[1]
        out_obj[...] = total[:ITERS, :TRAITS]

    stages = [t1, t2, t3, t4, t5, t6, t7, t8]
    for g in range(GROUPS):
        t0(g, 0)
    count = ITERS * len(stages)
    objective = [o1, o2, o3, o4, o5]
    last_t4 = (ITERS - 1) * len(stages) + 3
    lag = LAG
    for slot in range(count + lag * (GROUPS - 1)):
        for g in range(GROUPS):
            n = slot - lag * g
            if 0 <= n < count:
                stages[n % len(stages)](g, n // len(stages))
        if slot >= last_t4 + lag * (GROUPS - 1) and objective:
            objective.pop(0)()
    while objective:
        objective.pop(0)()
    for key in list(pending):
        settle(key)


LAG = 3


def on_device(genotypes, phenotype, beta_start, penalty, step_size):
    vmem, smem, hbm = (pl.BlockSpec(memory_space=m) for m in (pltpu.VMEM, pltpu.SMEM, pl.ANY))
    dma = pltpu.SemaphoreType.DMA

    def buf(*shape, dtype=F32):
        return pltpu.VMEM(shape, dtype)

    def pairs(*shape):
        return [dma(shape), dma(shape)]

    n = GROUPS
    return pl.pallas_call(
        kernel,
        name="lasso_steps",
        out_shape=(
            jax.ShapeDtypeStruct((LOCAL, COLS), F32),
            jax.ShapeDtypeStruct((ITERS, TRAITS), F32),
        ),
        in_specs=[smem, vmem, hbm, hbm, hbm],
        out_specs=(vmem, vmem),
        scratch_shapes=[
            buf(ROWS, COLS, dtype=BF16),
            buf(CHUNK, TRAITS),
            buf(X * C * n, R8, CHUNK),
            buf(LOCAL, COLS),
            buf(R8, 256),
            buf(Y, R8, 256),
            buf(Z, R8, 256),
            buf(X, R8, 256),
            buf(C, R8, 256),
            buf(n, X, C, 2 * R8, LO, dtype=BF16),
            buf(GT, COLS, dtype=BF16),
            buf(n, Y, GT, CHUNK),
            buf(n, Y - 1, GT, CHUNK),
            buf(n, Z, R8, CHUNK),
            buf(n, Z - 1, R8, CHUNK),
            buf(n, Z, R8, CHUNK),
            buf(n, GT, ROWS, dtype=BF16),
            buf(n, X, C, R8, COLS),
            buf(n, X, R8, COLS),
            buf(n, X, R8, COLS),
            buf(n, X - 1, R8, COLS),
            dma((6,)),
            *pairs(n, X),
            *pairs(n, X - 1),
            *pairs(n, Y - 1),
            *pairs(n, Z - 1),
            *pairs(n, Z - 1),
            *pairs(n, Y - 1),
            *pairs(n),
            *pairs(n, X - 1),
            *pairs(14),
        ],
        compiler_params=pltpu.CompilerParams(
            collective_id=1, has_side_effects=True, vmem_limit_bytes=40 * 1024 * 1024
        ),
        cost_estimate=pl.CostEstimate(flops=4 * 2 * ROWS * COLS * TRAITS, bytes_accessed=12000000, transcendentals=0),
    )(step_size, penalty.reshape(1, TRAITS), genotypes, phenotype, beta_start)


def solution(mesh):
    placed = (P("ind", "var"), P("ind", None), P("ind", "var"), P(), P())
    return jax.shard_map(
        on_device, mesh=mesh, in_specs=placed, out_specs=(P("ind", "var"), P()), check_vma=False
    )
```

time: 558 us -> 138 us (0.25)
  waiting for transfers between devices: 421 us -> 0 us
  Pallas kernels: 0 us -> 130 us
  blocking collectives: 79.1 us -> 0 us
  matrix products: 32.8 us -> 0 us
  between operations: 14.8 us -> 1.38 us
  other arithmetic: 6.96 us -> 0 us
    psum x4 -> x0, waiting for transfers between devices: 361 us -> none  [the longest x2 290 us: on_device(): predictor = lax.psum(partial_pred, 'var')]
    pallas_call x0 -> x1, Pallas kernels: none -> 130 us  [on_device(): pl.pallas_call(kernel, name='lasso_steps', out_shape=(jax.ShapeDtypeStruc...]
    psum x1 -> x0, blocking collectives: 79.1 us -> none  [on_device(): records.append(lax.psum(step_term, ('ind', 'var')))]
    all_gather x2 -> x0, waiting for transfers between devices: 60.1 us -> none  [on_device(): lax.all_gather(coef_half, 'ind', axis=0, tiled=True)]
    dot_general x4 -> x0, matrix products: 32.8 us -> none  [the longest x2 17.2 us: on_device(): lax.dot_general(genotypes, lax.all_gather(coef_half, 'ind', axis=0, tiled...]
  transfers between devices with their start and end apart: 6 -> 0, of which waited for: 5 -> 0; matrix products, arithmetic and copies ran while one was open for 0% -> 0% of each run, Pallas kernels for 0% -> 0%
where the time goes in v1:
time: 138 us
  Pallas kernels  130 us (94%)
  local copies, waits for them, and re-layouts  6.83 us (5%)
    pallas_call x1, Pallas kernels, on_device(): pl.pallas_call(kernel, name='lasso_steps', out_shape=(jax.ShapeDtypeStruc...  130 us
    unnamed x9, local copies, waits for them, and re-layouts  6.83 us

profile of v1, /device:TPU:1, one launch (start us, length us, event | category | flops | bytes accessed | tf_op | source)
XLA Modules:
  0.0 137.8 jit_solution(8194355125742132913)
XLA Ops:
  0.6 0.0 copy-start.2
  0.6 0.0 copy-start.1
  1.3 1.7 %copy.7.pheno = f32[1536,192]{1,0:T(8,128)S(1)} copy(f32[1536,192]{0,1:T(8,128)} %param.6) | data formatting | bytes 2359296 | tf_op args[1]
  3.1 0.0 copy-done.2
  3.1 0.0 copy-done.1
  3.1 0.0 copy-start
  3.1 3.8 %copy-done = bf16[1536,3200]{1,0:T(8,128)(2,1)S(1)} copy-done((bf16[1536,3200]{1,0:T(8,128)(2,1)S(1)}, bf16[1536,3200]{1,0:T(8,128)(2,1)}, u32[]{:S(2)}) %copy-start) | copy-done | bytes 9830424
  6.9 129.6 %lasso_steps.1 = (f32[24,3200]{1,0:T(8,128)S(1)}, f32[2,192]{1,0:T(2,128)S(1)}) custom-call(f32[1]{0:T(128)S(6)} %copy.10.step_ref, f32[1,192]{1,0:T(1,128)S(1)} %bitcast.1, bf16[1536,3200]{1,0:T(8,128)(2,1)S(1)} %copy-done, f32[1536,192]{1,0:T(8,128)S(1)} %copy.7.pheno, f32[24,3200]{1,0:T(8,128)S(1)} %copy-done.1), custom_call_target="tpu_custom_call" | custom-call | flops 7549747200 | bytes 12000000 | tf_op jit(solution)/shard_map/lasso_steps/pallas_call | solution.py:272
  136.5 0.7 copy.11
  137.3 0.6 copy.12
Async XLA Ops:
  0.6 2.5 %copy-start.2 = (f32[192]{0:T(256)S(1)}, f32[192]{0:T(256)}, u32[]{:S(2)}) copy-start(f32[192]{0:T(256)} %param.8) | copy-start | bytes 2308
  0.6 2.5 %copy-start.1 = (f32[24,3200]{1,0:T(8,128)S(1)}, f32[24,3200]{1,0:T(8,128)}, u32[]{:S(2)}) copy-start(f32[24,3200]{1,0:T(8,128)} %beta0.1) | copy-start | bytes 921604
  3.1 3.8 %copy-start = (bf16[1536,3200]{1,0:T(8,128)(2,1)S(1)}, bf16[1536,3200]{1,0:T(8,128)(2,1)}, u32[]{:S(2)}) copy-start(bf16[1536,3200]{1,0:T(8,128)(2,1)} %geno.1) | copy-start | bytes 29491204

commit v2 on v1

v2 whole, which is shorter than its diff:
```python
import functools

import jax
import jax.numpy as jnp
from jax import lax
from jax.experimental import pallas as pl
from jax.experimental.pallas import tpu as pltpu
from jax.sharding import PartitionSpec as P

ITERS = 2
X, C, Y, Z = 4, 2, 4, 8
GROUPS = 3
R8 = 8
ROWS, COLS = 1536, 3200
TRAITS = 192
LOCAL = TRAITS // (X * C)
GT = R8 * X * C
CHUNK = ROWS // Y
LO = 1664
HI = COLS - LO
PACK = 2 * R8
MESH = pl.DeviceIdType.MESH
F32, BF16 = jnp.float32, jnp.bfloat16
NT = (((1,), (1,)), ((), ()))
NN = (((1,), (0,)), ((), ()))
NEAR_Z = (4, 3, 5, 2, 6, 1, 7)
ORDER = (
    0, 0, 1, 0, 0, 1, 0, 0, 1, 1, 1, 2, 0, 1, 2, 2, 2, 0, 2, 1, 2, 0, 0, 1, 0, 0, 2, 0,
    1, 1, 1, 1, 2, 1, 0, 2, 2, 2, 2, 1, 2, 0, 0, 0, 0, 1, 0, 1, 2, 1, 0, 1, 1, 2, 1, 2,
    2, 2, 1, 2, 2, 0, 1, 2, 0, 1, 1, 1, 1, 2, 0, 0, 0, 1, 0, 2, 2, 2, 2, 0, 1, 2, 0, 2,
)


def kernel(
    step_ref, pen_ref, geno, pheno, beta0, out_beta, out_obj,
    g_buf, ph_t, bp, stat, stat_y, stat_z, stat_x, stat_c,
    cb, coef, pp, pph, ry, ryh, sz, rz, az, rt, keep, gp, pr, ps, psh, rx, rxh, asc,
    load_sem,
    agx_s, agx_r, rel_s, rel_r, rsy_s, rsy_r, rsz_s, rsz_r, agz_s, agz_r, agy_s, agy_r, pair_s, pair_r, rsx_s, rsx_r,
    ob_s, ob_r,
):
    ind, var = lax.axis_index("ind"), lax.axis_index("var")
    x, c = ind // C, ind % C
    y, z = var // Z, var % Z

    def at_x(k):
        return (((x + k) % X) * C + c, var)

    def at_y(k):
        return (ind, ((y + k) % Y) * Z + z)

    def at_z(k):
        return (ind, y * Z + (z + k) % Z)

    peer = (x * C + (1 - c), var)

    beta_loads = [
        pltpu.make_async_copy(beta0.at[:, :, pl.ds(0, LO)], bp.at[:, pl.ds(0, R8), :], load_sem.at[0]),
        pltpu.make_async_copy(beta0.at[:, :, pl.ds(LO, HI)], bp.at[:, pl.ds(R8, R8), pl.ds(0, HI)], load_sem.at[1]),
    ]
    for load in beta_loads:
        load.start()
    loads = []
    for n, k in enumerate((2, 1, 3, 0)):
        rows = pl.ds(pl.multiple_of(((y + k) % Y) * CHUNK, CHUNK), CHUNK)
        loads.append(pltpu.make_async_copy(geno.at[rows, :], g_buf.at[pl.ds(k * CHUNK, CHUNK), :], load_sem.at[3 + n]))
    for load in loads:
        load.start()
    own = pl.ds(pl.multiple_of(y * CHUNK, CHUNK), CHUNK)
    ph_load = pltpu.make_async_copy(pheno.at[:, own], ph_t, load_sem.at[2])
    ph_load.start()

    barrier = pltpu.get_barrier_semaphore()
    partners = [peer]
    partners += [at_x(k) for k in range(1, X)] + [at_y(k) for k in range(1, Y)] + [at_z(k) for k in range(1, Z)]
    for partner in partners:
        pl.semaphore_signal(barrier, inc=1, device_id=partner, device_id_type=MESH)

    scale = step_ref[0]
    bp[:, R8:, HI:] = jnp.zeros((GROUPS, R8, LO - HI), F32)
    for g in range(GROUPS):
        gp[g, :, :, R8:, HI:] = jnp.zeros((X, C, R8, LO - HI), F32)
    stat[...] = jnp.zeros_like(stat)

    pending = {}
    loaded = [False] * Y
    ph_loaded = []

    def send(key, src, dst, s_sem, r_sem, device):
        copy = pltpu.make_async_remote_copy(
            src_ref=src, dst_ref=dst, send_sem=s_sem, recv_sem=r_sem, device_id=device, device_id_type=MESH
        )
        copy.start()
        pending.setdefault(key, []).append(copy)

    def receive(key, one=None):
        copies = pending[key] if one is None else [pending[key][one]]
        for copy in copies:
            copy.wait_recv()

    def settle(key):
        for copy in pending.pop(key, []):
            copy.wait_send()

    for load in beta_loads:
        load.wait()
    pl.semaphore_wait(barrier, len(partners))

    def send_coef(g):
        settle(("agx", g))
        cb[g, 0, 0] = bp[g].astype(BF16)
        own = cb.at[g, 0, 0]
        for m, k in enumerate((2, 1, 3)):
            send(("agx", g), own, cb.at[g, k, 0], agx_s.at[g, m], agx_r.at[g, m], at_x(k))
        send(("agx", g), own, cb.at[g, 0, 1], agx_s.at[g, 3], agx_r.at[g, 3], peer)

    for g in range(GROUPS):
        send_coef(g)

    lane = lax.broadcasted_iota(jnp.int32, (LOCAL, TRAITS), 1)
    row = lax.broadcasted_iota(jnp.int32, (LOCAL, TRAITS), 0)
    pen_col = jnp.sum(jnp.where(lane == row + ind * LOCAL, pen_ref[...], 0.0), axis=1, keepdims=True)
    s_lane = lax.broadcasted_iota(jnp.int32, (LOCAL, 256), 1)
    s_row = lax.broadcasted_iota(jnp.int32, (LOCAL, 256), 0)

    def add_stat(it, first, column):
        hit = s_lane[: column.shape[0]] == s_row[: column.shape[0]] + first
        stat[it : it + 1, :] += jnp.sum(jnp.where(hit, column, 0.0), axis=0, keepdims=True) * (1.0 / (ROWS * X * C))

    def add_penalty(g, it):
        size = jnp.sum(jnp.abs(bp[g]), axis=1, keepdims=True)
        first = R8 * g
        add_stat(it, ind * LOCAL + first, pen_col[first : first + R8] * (size[:R8] + size[R8:]))

    def t1(g, it):
        for m, k in ((1, 1), (2, 3), (0, 2)):
            receive(("agx", g), m)
            send(("rel", g), cb.at[g, k, 0], cb.at[g, k, 1], rel_s.at[g, m], rel_r.at[g, m], peer)
        add_penalty(g, it)

    def t2(n, g, it):
        if n == 0:
            receive(("agx", g), 3)
            receive(("rel", g))
            settle(("rsy", g))
            for k in range(X):
                a, b = cb[g, k, 0].astype(F32), cb[g, k, 1].astype(F32)
                rows = slice(2 * R8 * k, 2 * R8 * k + 2 * R8)
                coef[g, rows, :LO] = jnp.concatenate([a[:R8], b[:R8]], axis=0).astype(BF16)
                coef[g, rows, LO:] = jnp.concatenate([a[R8:, :HI], b[R8:, :HI]], axis=0).astype(BF16)
        k = (2, 1, 3, 0)[n]
        if it == 0 and not loaded[n]:
            loads[n].wait()
            loaded[n] = True
        mine = lax.dot_general(
            coef[g], g_buf[CHUNK * k : CHUNK * k + CHUNK, :], NT, preferred_element_type=F32
        )
        if it:
            mine = mine - pp[g, k]
        if it and k:
            pph[g, k - 1] = mine.astype(BF16)
        else:
            pp[g, k] = mine
        if k:
            src, dst = (pph.at[g, k - 1], ryh.at[g, k - 1]) if it else (pp.at[g, k], ry.at[g, k - 1])
            send(("rsy", g), src, dst, rsy_s.at[g, k - 1], rsy_r.at[g, k - 1], at_y(k))

    def t3(g, it):
        receive(("rsy", g))
        settle(("rsz", g))
        total = pp[g, 0]
        for k in range(Y - 1):
            total = total + (ryh[g, k].astype(F32) if it else ry[g, k])
        sz[g] = total.reshape(Z, R8, CHUNK)
        for k in NEAR_Z:
            send(("rsz", g), sz.at[g, (z + k) % Z], rz.at[g, k - 1], rsz_s.at[g, k - 1], rsz_r.at[g, k - 1], at_z(k))

    def t4(g, it):
        if it == 0 and not ph_loaded:
            ph_load.wait()
            ph_loaded.append(True)
        receive(("rsz", g))
        settle(("agz", g))
        total = sz[g, z]
        for k in range(Z - 1):
            total = total + rz[g, k]
        if it:
            total = total + keep[g]
        else:
            keep[g] = total
        k, f = z // C, z % C
        owner = ((x - k + X) % X) * C + (c + f) % C
        first = owner * LOCAL + R8 * g
        residual = ph_t[pl.ds(pl.multiple_of(first, R8), R8), :] - total
        az[g, z] = residual
        for k in NEAR_Z:
            send(("agz", g), az.at[g, z], az.at[g, z], agz_s.at[g, k - 1], agz_r.at[g, k - 1], at_z(k))
        add_stat(it, first, 0.5 * jnp.sum(residual * residual, axis=1, keepdims=True))

    def t5(g, it):
        receive(("agz", g))
        settle(("agy", g))
        rt[g, :, :CHUNK] = az[g].reshape(GT, CHUNK).astype(BF16)
        for k in (2, 1, 3):
            m = (Y - k) % Y
            send(
                ("agy", g), rt.at[g, :, pl.ds(0, CHUNK)], rt.at[g, :, pl.ds(m * CHUNK, CHUNK)],
                agy_s.at[g, k - 1], agy_r.at[g, k - 1], at_y(k),
            )

    def t6(n, g, it):
        if n == 0:
            receive(("agy", g))
            settle(("pair", g))
        row, a, b = ((0, 0, 896), (0, 896, LO), (1, 0, 768), (1, 768, HI))[n]
        part = lax.dot_general(rt[g], g_buf[:, LO * row + a : LO * row + b], NN, preferred_element_type=F32)
        gp[g, :, :, R8 * row : R8 * row + R8, a:b] = part.reshape(X, C, R8, b - a)
        if n == 3:
            send(("pair", g), gp.at[g, :, 1], pr.at[g], pair_s.at[g], pair_r.at[g], peer)

    def t7(g, it):
        receive(("pair", g))
        settle(("rel", g))
        settle(("rsx", g))
        for k in (2, 1, 3, 0):
            mine = gp[g, k, 0] + pr[g, k]
            if it:
                mine = mine - ps[g, k]
            if it and k:
                psh[g, k - 1] = mine.astype(BF16)
            else:
                ps[g, k] = mine
            if k:
                src, dst = (psh.at[g, k - 1], rxh.at[g, k - 1]) if it else (ps.at[g, k], rx.at[g, k - 1])
                send(("rsx", g), src, dst, rsx_s.at[g, k - 1], rsx_r.at[g, k - 1], at_x(X - k))

    def t8(g, it):
        receive(("rsx", g))
        ascent = ps[g, 0]
        for k in range(X - 1):
            ascent = ascent + (rxh[g, k].astype(F32) if it else rx[g, k])
        if it:
            ascent = ascent + asc[g]
        else:
            asc[g] = ascent
        rows = slice(R8 * g, R8 * g + R8)
        moved = bp[g] + scale * ascent
        bound = jnp.concatenate([pen_col[rows], pen_col[rows]], axis=0) * scale
        updated = moved - jnp.clip(moved, -bound, bound)
        if it == ITERS - 1:
            out_beta[rows, :LO] = updated[:R8]
            out_beta[rows, LO:] = updated[R8:, :HI]
        else:
            bp[g] = updated
            send_coef(g)

    def o1():
        stat_y[y] = stat[...]
        for k in range(1, Y):
            send("oy", stat_y.at[y], stat_y.at[y], ob_s.at[k - 1], ob_r.at[k - 1], at_y(k))

    def o2():
        receive("oy")
        stat_z[z] = stat_y[0] + stat_y[1] + stat_y[2] + stat_y[3]
        for k in range(1, Z):
            send("oz", stat_z.at[z], stat_z.at[z], ob_s.at[2 + k], ob_r.at[2 + k], at_z(k))

    def o3():
        receive("oz")
        total = stat_z[0]
        for k in range(1, Z):
            total = total + stat_z[k]
        stat_x[x] = total
        for k in range(1, X):
            send("ox", stat_x.at[x], stat_x.at[x], ob_s.at[9 + k], ob_r.at[9 + k], at_x(k))

    def o4():
        receive("ox")
        stat_c[c] = stat_x[0] + stat_x[1] + stat_x[2] + stat_x[3]
        send("oc", stat_c.at[c], stat_c.at[c], ob_s.at[13], ob_r.at[13], peer)

    def o5():
        receive("oc")
        out_obj[...] = (stat_c[0] + stat_c[1])[:ITERS, :TRAITS]

    stages = []
    for it in range(ITERS):
        stages += [(t1, it)] + [(functools.partial(t2, n), it) for n in range(Y)]
        stages += [(t3, it), (t4, it), (t5, it)] + [(functools.partial(t6, n), it) for n in range(4)] + [(t7, it), (t8, it)]
    objective = [o1, o2, o3, o4, o5]
    done = [0] * GROUPS
    for place, g in enumerate(ORDER):
        stage, it = stages[done[g]]
        stage(g, it)
        done[g] += 1
        if min(done) > stages.index((t4, ITERS - 1)) and objective and place % 3 == 0:
            objective.pop(0)()
    for step in objective:
        step()
    for key in list(pending):
        settle(key)


def on_device(genotypes, phenotype, beta_start, penalty, step_size):
    vmem, smem, hbm = (pl.BlockSpec(memory_space=m) for m in (pltpu.VMEM, pltpu.SMEM, pl.ANY))
    dma = pltpu.SemaphoreType.DMA

    def buf(*shape, dtype=F32):
        return pltpu.VMEM(shape, dtype)

    def pairs(*shape):
        return [dma(shape), dma(shape)]

    n = GROUPS
    return pl.pallas_call(
        kernel,
        name="lasso_steps",
        out_shape=(
            jax.ShapeDtypeStruct((LOCAL, COLS), F32),
            jax.ShapeDtypeStruct((ITERS, TRAITS), F32),
        ),
        in_specs=[smem, vmem, hbm, hbm, hbm],
        out_specs=(vmem, vmem),
        scratch_shapes=[
            buf(ROWS, COLS, dtype=BF16),
            buf(TRAITS, CHUNK),
            buf(n, PACK, LO),
            buf(R8, 256),
            buf(Y, R8, 256),
            buf(Z, R8, 256),
            buf(X, R8, 256),
            buf(C, R8, 256),
            buf(n, X, C, PACK, LO, dtype=BF16),
            buf(n, GT, COLS, dtype=BF16),
            buf(n, Y, GT, CHUNK),
            buf(n, Y - 1, GT, CHUNK, dtype=BF16),
            buf(n, Y - 1, GT, CHUNK),
            buf(n, Y - 1, GT, CHUNK, dtype=BF16),
            buf(n, Z, R8, CHUNK),
            buf(n, Z - 1, R8, CHUNK),
            buf(n, Z, R8, CHUNK),
            buf(n, GT, ROWS, dtype=BF16),
            buf(n, R8, CHUNK),
            buf(n, X, C, PACK, LO),
            buf(n, X, PACK, LO),
            buf(n, X, PACK, LO),
            buf(n, X - 1, PACK, LO, dtype=BF16),
            buf(n, X - 1, PACK, LO),
            buf(n, X - 1, PACK, LO, dtype=BF16),
            buf(n, PACK, LO),
            dma((7,)),
            *pairs(n, X),
            *pairs(n, X - 1),
            *pairs(n, Y - 1),
            *pairs(n, Z - 1),
            *pairs(n, Z - 1),
            *pairs(n, Y - 1),
            *pairs(n),
            *pairs(n, X - 1),
            *pairs(14),
        ],
        compiler_params=pltpu.CompilerParams(
            collective_id=1, has_side_effects=True, vmem_limit_bytes=55 * 1024 * 1024
        ),
        cost_estimate=pl.CostEstimate(flops=4 * 2 * ROWS * COLS * TRAITS, bytes_accessed=12000000, transcendentals=0),
    )(step_size, penalty.reshape(1, TRAITS), genotypes, phenotype.T, beta_start.reshape(n, R8, COLS))


def solution(mesh):
    placed = (P("ind", "var"), P("ind", None), P("ind", "var"), P(), P())
    return jax.shard_map(
        on_device, mesh=mesh, in_specs=placed, out_specs=(P("ind", "var"), P()), check_vma=False
    )
```

time: 138 us -> 114 us (0.83)
  Pallas kernels: 130 us -> 109 us
  local copies, waits for them, and re-layouts: 6.83 us -> 2.96 us
    pallas_call x1, Pallas kernels: 130 us -> 109 us  [on_device(): pl.pallas_call(kernel, name='lasso_steps', out_shape=(jax.ShapeDtypeStruc...]
    unnamed x9 -> x2, local copies, waits for them, and re-layouts: 6.83 us -> 2.96 us
where the time goes in v2:
time: 114 us
  Pallas kernels  109 us (96%)
  local copies, waits for them, and re-layouts  2.96 us (3%)
  between operations  1.29 us (1%)
    pallas_call x1, Pallas kernels, on_device(): pl.pallas_call(kernel, name='lasso_steps', out_shape=(jax.ShapeDtypeStruc...  109 us
    unnamed x2, local copies, waits for them, and re-layouts  2.96 us

profile of v2, /device:TPU:1, one launch (start us, length us, event | category | flops | bytes accessed | tf_op | source)
XLA Modules:
  0.0 113.5 jit_solution(18342872004692387678)
XLA Ops:
  1.3 109.3 %lasso_steps.1 = (f32[24,3200]{1,0:T(8,128)}, f32[2,192]{1,0:T(2,128)}) custom-call(f32[1]{0:T(128)S(6)} %copy.9.step_ref, f32[1,192]{1,0:T(1,128)} %bitcast.5, bf16[1536,3200]{1,0:T(8,128)(2,1)} %geno.1, f32[192,1536]{1,0:T(8,128)} %bitcast.3, f32[3,8,3200]{2,1,0:T(8,128)} %bitcast.4), custom_call_target="tpu_custom_call" | custom-call | flops 7549747200 | bytes 12000000 | tf_op jit(solution)/shard_map/lasso_steps/pallas_call | solution.py:315
  110.6 1.7 %copy.10 = f32[24,3200]{1,0:T(8,128)} copy(f32[24,3200]{1,0:T(8,128)} %get-tuple-element.4) | data formatting | bytes 614400
  112.3 1.3 %copy.11 = f32[2,192]{1,0:T(2,128)} copy(f32[2,192]{1,0:T(2,128)} %get-tuple-element.5) | data formatting | bytes 3072

commit v3 on v2

--- a/solution.py
+++ b/solution.py
@@ -19,15 +19,16 @@
 LO = 1664
 HI = COLS - LO
 PACK = 2 * R8
+CUTS = ((0, 896), (896, LO))
 MESH = pl.DeviceIdType.MESH
 F32, BF16 = jnp.float32, jnp.bfloat16
 NT = (((1,), (1,)), ((), ()))
 NN = (((1,), (0,)), ((), ()))
 NEAR_Z = (4, 3, 5, 2, 6, 1, 7)
 ORDER = (
-    0, 0, 1, 0, 0, 1, 0, 0, 1, 1, 1, 2, 0, 1, 2, 2, 2, 0, 2, 1, 2, 0, 0, 1, 0, 0, 2, 0,
-    1, 1, 1, 1, 2, 1, 0, 2, 2, 2, 2, 1, 2, 0, 0, 0, 0, 1, 0, 1, 2, 1, 0, 1, 1, 2, 1, 2,
-    2, 2, 1, 2, 2, 0, 1, 2, 0, 1, 1, 1, 1, 2, 0, 0, 0, 1, 0, 2, 2, 2, 2, 0, 1, 2, 0, 2,
+    0, 0, 1, 0, 1, 0, 0, 0, 2, 2, 1, 0, 2, 2, 1, 2, 2, 0, 1, 1, 2, 1, 0, 2, 0, 0, 0, 1, 0, 0, 2, 0, 1, 0,
+    2, 2, 2, 0, 2, 2, 0, 1, 2, 1, 0, 1, 1, 1, 2, 0, 2, 1, 0, 1, 0, 0, 2, 2, 0, 1, 2, 1, 2, 2, 2, 1, 0, 2,
+    1, 1, 1, 1, 0, 1, 2, 0, 0, 0, 0, 1, 0, 0, 2, 0, 1, 0, 2, 2, 2, 2, 2, 1, 1, 2, 1, 1, 1, 2, 1, 2, 1, 1,
 )
 
 
@@ -64,8 +65,6 @@
     for n, k in enumerate((2, 1, 3, 0)):
         rows = pl.ds(pl.multiple_of(((y + k) % Y) * CHUNK, CHUNK), CHUNK)
         loads.append(pltpu.make_async_copy(geno.at[rows, :], g_buf.at[pl.ds(k * CHUNK, CHUNK), :], load_sem.at[3 + n]))
-    for load in loads:
-        load.start()
     own = pl.ds(pl.multiple_of(y * CHUNK, CHUNK), CHUNK)
     ph_load = pltpu.make_async_copy(pheno.at[:, own], ph_t, load_sem.at[2])
     ph_load.start()
@@ -106,16 +105,21 @@
         load.wait()
     pl.semaphore_wait(barrier, len(partners))
 
-    def send_coef(g):
-        settle(("agx", g))
-        cb[g, 0, 0] = bp[g].astype(BF16)
-        own = cb.at[g, 0, 0]
+    def send_coef(n, g):
+        settle(("agx", g, n))
+        a, b = CUTS[n]
+        cols = pl.ds(a, b - a)
+        cb[g, 0, 0, :, a:b] = bp[g, :, a:b].astype(BF16)
+        own = cb.at[g, 0, 0, :, cols]
         for m, k in enumerate((2, 1, 3)):
-            send(("agx", g), own, cb.at[g, k, 0], agx_s.at[g, m], agx_r.at[g, m], at_x(k))
-        send(("agx", g), own, cb.at[g, 0, 1], agx_s.at[g, 3], agx_r.at[g, 3], peer)
+            send(("agx", g, n), own, cb.at[g, k, 0, :, cols], agx_s.at[g, n, m], agx_r.at[g, n, m], at_x(k))
+        send(("agx", g, n), own, cb.at[g, 0, 1, :, cols], agx_s.at[g, n, 3], agx_r.at[g, n, 3], peer)
 
     for g in range(GROUPS):
-        send_coef(g)
+        for n in range(len(CUTS)):
+            send_coef(n, g)
+    for load in loads:
+        load.start()
 
     lane = lax.broadcasted_iota(jnp.int32, (LOCAL, TRAITS), 1)
     row = lax.broadcasted_iota(jnp.int32, (LOCAL, TRAITS), 0)
@@ -132,16 +136,21 @@
         first = R8 * g
         add_stat(it, ind * LOCAL + first, pen_col[first : first + R8] * (size[:R8] + size[R8:]))
 
-    def t1(g, it):
+    def t1(n, g, it):
+        a, b = CUTS[n]
+        cols = pl.ds(a, b - a)
         for m, k in ((1, 1), (2, 3), (0, 2)):
-            receive(("agx", g), m)
-            send(("rel", g), cb.at[g, k, 0], cb.at[g, k, 1], rel_s.at[g, m], rel_r.at[g, m], peer)
-        add_penalty(g, it)
+            receive(("agx", g, n), m)
+            src, dst = cb.at[g, k, 0, :, cols], cb.at[g, k, 1, :, cols]
+            send(("rel", g, n), src, dst, rel_s.at[g, n, m], rel_r.at[g, n, m], peer)
+        if n == 1:
+            add_penalty(g, it)
 
     def t2(n, g, it):
         if n == 0:
-            receive(("agx", g), 3)
-            receive(("rel", g))
+            for part in range(len(CUTS)):
+                receive(("agx", g, part), 3)
+                receive(("rel", g, part))
             settle(("rsy", g))
             for k in range(X):
                 a, b = cb[g, k, 0].astype(F32), cb[g, k, 1].astype(F32)
@@ -211,48 +220,58 @@
     def t6(n, g, it):
         if n == 0:
             receive(("agy", g))
-            settle(("pair", g))
-        row, a, b = ((0, 0, 896), (0, 896, LO), (1, 0, 768), (1, 768, HI))[n]
-        part = lax.dot_general(rt[g], g_buf[:, LO * row + a : LO * row + b], NN, preferred_element_type=F32)
-        gp[g, :, :, R8 * row : R8 * row + R8, a:b] = part.reshape(X, C, R8, b - a)
-        if n == 3:
-            send(("pair", g), gp.at[g, :, 1], pr.at[g], pair_s.at[g], pair_r.at[g], peer)
-
-    def t7(g, it):
-        receive(("pair", g))
-        settle(("rel", g))
-        settle(("rsx", g))
+        row, part = n % 2, n // 2
+        a, b = CUTS[part]
+        high = min(b, HI) if row else b
+        if row == 0:
+            settle(("pair", g, part))
+        grad = lax.dot_general(rt[g], g_buf[:, LO * row + a : LO * row + high], NN, preferred_element_type=F32)
+        gp[g, :, :, R8 * row : R8 * row + R8, a:high] = grad.reshape(X, C, R8, high - a)
+        if row:
+            cols = pl.ds(a, b - a)
+            src, dst = gp.at[g, :, 1, :, cols], pr.at[g, :, :, cols]
+            send(("pair", g, part), src, dst, pair_s.at[g, part], pair_r.at[g, part], peer)
+
+    def t7(n, g, it):
+        a, b = CUTS[n]
+        cols = pl.ds(a, b - a)
+        receive(("pair", g, n))
+        settle(("rel", g, n))
+        settle(("rsx", g, n))
         for k in (2, 1, 3, 0):
-            mine = gp[g, k, 0] + pr[g, k]
+            mine = gp[g, k, 0, :, a:b] + pr[g, k, :, a:b]
             if it:
-                mine = mine - ps[g, k]
+                mine = mine - ps[g, k, :, a:b]
             if it and k:
-                psh[g, k - 1] = mine.astype(BF16)
+                psh[g, k - 1, :, a:b] = mine.astype(BF16)
             else:
-                ps[g, k] = mine
+                ps[g, k, :, a:b] = mine
             if k:
-                src, dst = (psh.at[g, k - 1], rxh.at[g, k - 1]) if it else (ps.at[g, k], rx.at[g, k - 1])
-                send(("rsx", g), src, dst, rsx_s.at[g, k - 1], rsx_r.at[g, k - 1], at_x(X - k))
-
-    def t8(g, it):
-        receive(("rsx", g))
-        ascent = ps[g, 0]
+                src = psh.at[g, k - 1, :, cols] if it else ps.at[g, k, :, cols]
+                dst = (rxh if it else rx).at[g, k - 1, :, cols]
+                send(("rsx", g, n), src, dst, rsx_s.at[g, n, k - 1], rsx_r.at[g, n, k - 1], at_x(X - k))
+
+    def t8(n, g, it):
+        a, b = CUTS[n]
+        high = min(b, HI)
+        receive(("rsx", g, n))
+        ascent = ps[g, 0, :, a:b]
         for k in range(X - 1):
-            ascent = ascent + (rxh[g, k].astype(F32) if it else rx[g, k])
+            ascent = ascent + (rxh[g, k, :, a:b].astype(F32) if it else rx[g, k, :, a:b])
         if it:
-            ascent = ascent + asc[g]
+            ascent = ascent + asc[g, :, a:b]
         else:
-            asc[g] = ascent
+            asc[g, :, a:b] = ascent
         rows = slice(R8 * g, R8 * g + R8)
-        moved = bp[g] + scale * ascent
+        moved = bp[g, :, a:b] + scale * ascent
         bound = jnp.concatenate([pen_col[rows], pen_col[rows]], axis=0) * scale
         updated = moved - jnp.clip(moved, -bound, bound)
         if it == ITERS - 1:
-            out_beta[rows, :LO] = updated[:R8]
-            out_beta[rows, LO:] = updated[R8:, :HI]
+            out_beta[rows, a:b] = updated[:R8]
+            out_beta[rows, LO + a : LO + high] = updated[R8:, : high - a]
         else:
-            bp[g] = updated
-            send_coef(g)
+            bp[g, :, a:b] = updated
+            send_coef(n, g)
 
     def o1():
         stat_y[y] = stat[...]
@@ -285,8 +304,8 @@
 
     stages = []
     for it in range(ITERS):
-        stages += [(t1, it)] + [(functools.partial(t2, n), it) for n in range(Y)]
-        stages += [(t3, it), (t4, it), (t5, it)] + [(functools.partial(t6, n), it) for n in range(4)] + [(t7, it), (t8, it)]
+        for stage, parts in ((t1, 2), (t2, Y), (t3, 0), (t4, 0), (t5, 0), (t6, 4), (t7, 2), (t8, 2)):
+            stages += [(functools.partial(stage, n), it) for n in range(parts)] or [(stage, it)]
     objective = [o1, o2, o3, o4, o5]
     done = [0] * GROUPS
     for place, g in enumerate(ORDER):
@@ -311,13 +330,13 @@
     def pairs(*shape):
         return [dma(shape), dma(shape)]
 
-    n = GROUPS
+    n, m = GROUPS, len(CUTS)
     return pl.pallas_call(
         kernel,
         name="lasso_steps",
         out_shape=(
-            jax.ShapeDtypeStruct((LOCAL, COLS), F32),
-            jax.ShapeDtypeStruct((ITERS, TRAITS), F32),
+            pltpu.VMEM((LOCAL, COLS), F32),
+            pltpu.VMEM((ITERS, TRAITS), F32),
         ),
         in_specs=[smem, vmem, hbm, hbm, hbm],
         out_specs=(vmem, vmem),
@@ -349,14 +368,14 @@
             buf(n, X - 1, PACK, LO, dtype=BF16),
             buf(n, PACK, LO),
             dma((7,)),
-            *pairs(n, X),
-            *pairs(n, X - 1),
+            *pairs(n, m, X),
+            *pairs(n, m, X - 1),
             *pairs(n, Y - 1),
             *pairs(n, Z - 1),
             *pairs(n, Z - 1),
             *pairs(n, Y - 1),
-            *pairs(n),
-            *pairs(n, X - 1),
+            *pairs(n, m),
+            *pairs(n, m, X - 1),
             *pairs(14),
         ],
         compiler_params=pltpu.CompilerParams(

time: 114 us -> 110 us (0.965)
  local copies, waits for them, and re-layouts: 2.96 us -> 1.3 us
    pallas_call x1, Pallas kernels: 109 us -> 108 us  [on_device(): pl.pallas_call(kernel, name='lasso_steps', out_shape=(pltpu.VMEM((LOCAL,...]
    unnamed x2, local copies, waits for them, and re-layouts: 2.96 us -> 1.3 us
where the time goes in v3:
time: 110 us
  Pallas kernels  108 us (98%)
  local copies, waits for them, and re-layouts  1.3 us (1%)
  between operations  1.29 us (1%)
    pallas_call x1, Pallas kernels, on_device(): pl.pallas_call(kernel, name='lasso_steps', out_shape=(pltpu.VMEM((LOCAL,...  108 us

profile of v3, /device:TPU:1, one launch (start us, length us, event | category | flops | bytes accessed | tf_op | source)
XLA Modules:
  0.0 110.2 jit_solution(16803837049849562972)
XLA Ops:
  1.3 107.6 %lasso_steps.1 = (f32[24,3200]{1,0:T(8,128)S(1)}, f32[2,192]{1,0:T(2,128)S(1)}) custom-call(f32[1]{0:T(128)S(6)} %copy.11.step_ref, f32[1,192]{1,0:T(1,128)} %bitcast.5, bf16[1536,3200]{1,0:T(8,128)(2,1)} %geno.1, f32[192,1536]{1,0:T(8,128)} %bitcast.3, f32[3,8,3200]{2,1,0:T(8,128)} %bitcast.4), custom_call_target="tpu_custom_call" | custom-call | flops 7549747200 | bytes 12000000 | tf_op jit(solution)/shard_map/lasso_steps/pallas_call | solution.py:334
  108.9 0.7 copy.9
  109.6 0.6 copy.10

commit v4 on v3

--- a/solution.py
+++ b/solution.py
@@ -92,13 +92,26 @@
         copy.start()
         pending.setdefault(key, []).append(copy)
 
+    def bulk(name, g):
+        ref, s_sem, r_sem = (rz.at[g], rsz_s, rsz_r) if name == "rsz" else (az.at[g, pl.ds(0, Z - 1)], agz_s, agz_r)
+        return pltpu.make_async_remote_copy(
+            src_ref=ref, dst_ref=ref, send_sem=s_sem.at[g], recv_sem=r_sem.at[g], device_id=at_z(1), device_id_type=MESH
+        )
+
     def receive(key, one=None):
+        if key[0] in ("rsz", "agz"):
+            bulk(*key).wait_recv()
+            return
         copies = pending[key] if one is None else [pending[key][one]]
         for copy in copies:
             copy.wait_recv()
 
     def settle(key):
-        for copy in pending.pop(key, []):
+        copies = pending.pop(key, [])
+        if copies and key[0] in ("rsz", "agz"):
+            bulk(*key).wait_send()
+            return
+        for copy in copies:
             copy.wait_send()
 
     for load in beta_loads:
@@ -182,7 +195,7 @@
             total = total + (ryh[g, k].astype(F32) if it else ry[g, k])
         sz[g] = total.reshape(Z, R8, CHUNK)
         for k in NEAR_Z:
-            send(("rsz", g), sz.at[g, (z + k) % Z], rz.at[g, k - 1], rsz_s.at[g, k - 1], rsz_r.at[g, k - 1], at_z(k))
+            send(("rsz", g), sz.at[g, (z + k) % Z], rz.at[g, k - 1], rsz_s.at[g], rsz_r.at[g], at_z(k))
 
     def t4(g, it):
         if it == 0 and not ph_loaded:
@@ -203,7 +216,7 @@
         residual = ph_t[pl.ds(pl.multiple_of(first, R8), R8), :] - total
         az[g, z] = residual
         for k in NEAR_Z:
-            send(("agz", g), az.at[g, z], az.at[g, z], agz_s.at[g, k - 1], agz_r.at[g, k - 1], at_z(k))
+            send(("agz", g), az.at[g, z], az.at[g, z], agz_s.at[g], agz_r.at[g], at_z(k))
         add_stat(it, first, 0.5 * jnp.sum(residual * residual, axis=1, keepdims=True))
 
     def t5(g, it):
@@ -371,8 +384,8 @@
             *pairs(n, m, X),
             *pairs(n, m, X - 1),
             *pairs(n, Y - 1),
-            *pairs(n, Z - 1),
-            *pairs(n, Z - 1),
+            *pairs(n),
+            *pairs(n),
             *pairs(n, Y - 1),
             *pairs(n, m),
             *pairs(n, m, X - 1),

time: 110 us -> 110 us (level)
  no operation moved by 1% of the time
where the time goes in v4:
time: 110 us
  Pallas kernels  107 us (97%)
  local copies, waits for them, and re-layouts  1.3 us (1%)
  between operations  1.29 us (1%)
    pallas_call x1, Pallas kernels, on_device(): pl.pallas_call(kernel, name='lasso_steps', out_shape=(pltpu.VMEM((LOCAL,...  107 us

profile of v4, /device:TPU:1, one launch (start us, length us, event | category | flops | bytes accessed | tf_op | source)
XLA Modules:
  0.0 109.8 jit_solution(4715010700319836411)
XLA Ops:
  1.3 107.2 %lasso_steps.1 = (f32[24,3200]{1,0:T(8,128)S(1)}, f32[2,192]{1,0:T(2,128)S(1)}) custom-call(f32[1]{0:T(128)S(6)} %copy.11.step_ref, f32[1,192]{1,0:T(1,128)} %bitcast.5, bf16[1536,3200]{1,0:T(8,128)(2,1)} %geno.1, f32[192,1536]{1,0:T(8,128)} %bitcast.3, f32[3,8,3200]{2,1,0:T(8,128)} %bitcast.4), custom_call_target="tpu_custom_call" | custom-call | flops 7549747200 | bytes 12000000 | tf_op jit(solution)/shard_map/lasso_steps/pallas_call | solution.py:347
  108.5 0.7 copy.9
  109.2 0.6 copy.10

commit v5 on v4

--- a/solution.py
+++ b/solution.py
@@ -152,10 +152,11 @@
     def t1(n, g, it):
         a, b = CUTS[n]
         cols = pl.ds(a, b - a)
-        for m, k in ((1, 1), (2, 3), (0, 2)):
+        for m in range(X - 1):
             receive(("agx", g, n), m)
-            src, dst = cb.at[g, k, 0, :, cols], cb.at[g, k, 1, :, cols]
-            send(("rel", g, n), src, dst, rel_s.at[g, n, m], rel_r.at[g, n, m], peer)
+        others = pl.ds(1, X - 1)
+        src, dst = cb.at[g, others, 0, :, cols], cb.at[g, others, 1, :, cols]
+        send(("rel", g, n), src, dst, rel_s.at[g, n], rel_r.at[g, n], peer)
         if n == 1:
             add_penalty(g, it)
 
@@ -382,7 +383,7 @@
             buf(n, PACK, LO),
             dma((7,)),
             *pairs(n, m, X),
-            *pairs(n, m, X - 1),
+            *pairs(n, m),
             *pairs(n, Y - 1),
             *pairs(n),
             *pairs(n),

time: 110 us -> 110 us (level)
  no operation moved by 1% of the time
where the time goes in v5:
time: 110 us
  Pallas kernels  107 us (97%)
  local copies, waits for them, and re-layouts  1.3 us (1%)
  between operations  1.29 us (1%)
    pallas_call x1, Pallas kernels, on_device(): pl.pallas_call(kernel, name='lasso_steps', out_shape=(pltpu.VMEM((LOCAL,...  107 us

profile of v5, /device:TPU:1, one launch (start us, length us, event | category | flops | bytes accessed | tf_op | source)
XLA Modules:
  0.0 109.6 jit_solution(13423987614033929747)
XLA Ops:
  1.3 107.0 %lasso_steps.1 = (f32[24,3200]{1,0:T(8,128)S(1)}, f32[2,192]{1,0:T(2,128)S(1)}) custom-call(f32[1]{0:T(128)S(6)} %copy.11.step_ref, f32[1,192]{1,0:T(1,128)} %bitcast.5, bf16[1536,3200]{1,0:T(8,128)(2,1)} %geno.1, f32[192,1536]{1,0:T(8,128)} %bitcast.3, f32[3,8,3200]{2,1,0:T(8,128)} %bitcast.4), custom_call_target="tpu_custom_call" | custom-call | flops 7549747200 | bytes 12000000 | tf_op jit(solution)/shard_map/lasso_steps/pallas_call | solution.py:348
  108.3 0.7 copy.9
  109.0 0.6 copy.10
